TPU v7x, 512 devices: a whole 4x4x16 slice. The times are simulated.
512 devices in a mesh: tile: 32 (over y, x, core), aux: 16 (over z).
Axes of the slice: x: 4, y: 4, z: 16, core: 2. Of those that a mesh axis runs over, the one named last changes fastest.
Arguments:
- amplitudes: bfloat16 [128, 128, 128], P('tile'), may hold values from -6 to 6
- df_factors: bfloat16 [1536, 3072], P('aux'), may hold values from -0.15625 to 0.15625
- out_tiles: int32 [1024], P(('tile', 'aux')), may hold values from 0 to 23
- pair_col: int32 [1024, 16], P(('tile', 'aux')), may hold values from 0 to 23
- pair_amp: int32 [1024, 16], replicated, may hold values from 0 to 127, as said below
Outputs:
- residual: bfloat16 [1024, 128, 128], P(('tile', 'aux'))
Inputs may be any that keep to these rules, and one draw needn't show every extreme that they name: `pair_amp`: among the 32 entries of the output tiles of one device, no owner occurs more than 2 times, and in every device's entries at least one owner occurs exactly 2 times (several may).
All inputs are finite; a program needn't handle non-finite values.
Results may differ from a plain program's by a relative error of at most 0.0049.
Values may be sent and summed in bfloat16 or wider, within the bound.
A program may use at most 128 MiB of HBM per device.

v0:
```python
import jax
import jax.numpy as jnp
from jax import lax
from jax.sharding import PartitionSpec as P


def body(amplitudes, df_factors, out_tiles, pair_col, pair_amp):
    n_tile = lax.axis_size("tile")
    n_aux = lax.axis_size("aux")
    me_tile = lax.axis_index("tile")
    me_aux = lax.axis_index("aux")
    out_count = out_tiles.shape[0]
    pair_count = pair_col.shape[1]
    tile_size = amplitudes.shape[1]
    pair_width = df_factors.shape[1]
    ptiles = pair_width // tile_size
    per_device = out_count * pair_count
    shard_rows = lax.all_gather(df_factors, "aux", axis=0, tiled=True)
    columns = shard_rows.reshape(shard_rows.shape[0], ptiles, tile_size)
    right_side = jnp.take(columns, out_tiles, axis=1)
    assembled = jnp.einsum(
        "qv,qob->ovb", shard_rows, right_side, preferred_element_type=jnp.float32
    )
    gram_rows = assembled.reshape(out_count, ptiles, tile_size, tile_size)
    panels = jnp.take_along_axis(gram_rows, pair_col[:, :, None, None], axis=1).astype(jnp.bfloat16)
    everyone = pair_amp.reshape(n_tile, n_aux, per_device)
    my_lists = lax.dynamic_index_in_dim(everyone, me_aux, 1, keepdims=False)
    own_list = lax.dynamic_index_in_dim(my_lists, me_tile, 0, keepdims=False)
    all_tiles = lax.all_gather(amplitudes, "tile", axis=0, tiled=True)
    picked = jnp.take(all_tiles, own_list, axis=0)
    stacked = picked.reshape(out_count, pair_count, tile_size, tile_size)
    result = jnp.einsum("okac,okcb->oab", stacked, panels, preferred_element_type=jnp.float32)
    return result.astype(jnp.bfloat16)


def solution(mesh):
    in_specs = (
        P("tile", None, None),
        P("aux", None),
        P(("tile", "aux")),
        P(("tile", "aux"), None),
        P(),
    )
    out_specs = P(("tile", "aux"), None, None)
    return jax.shard_map(body, mesh=mesh, in_specs=in_specs, out_specs=out_specs, check_vma=False)
```

profile of v0, /device:TPU:1, one launch (start us, length us, event | category | flops | bytes accessed | tf_op | source)
XLA Modules:
  0.0 227.0 jit_solution(2826224950712772218)
XLA Ops:
  6.5 0.0 all-gather.3.cloned.1.call-start
  6.5 0.7 all-gather.3.cloned.1.call-update
  7.3 0.0 all-gather.5.cloned.1.call-start
  7.3 0.7 all-gather.5.cloned.1.call-update
  8.0 0.7 bitcast_or_fusion
  8.7 0.1 reshape.94
  8.8 1.0 copy.11
  9.8 0.1 reshape.74
  10.0 0.1 squeeze.8
  10.1 0.7 compare_select_fusion.2
  10.8 0.7 compare_and_fusion
  11.4 0.7 compare_and_fusion.1
  12.1 65.5 %all-gather.3.cloned.1.call-done = bf16[128,128,128]{2,1,0:T(8,128)(2,1)} async-done(((bf16[4,128,128]{2,1,0:T(8,128)(2,1)}), bf16[128,128,128]{2,1,0:T(8,128)(2,1)}) %all-gather.3.cloned.1.call-update) | async-done | bytes 4194320 | tf_op jit(solution)/shard_map/all_gather | solution.py:29
  77.6 3.9 %gather_fusion = bf16[32,128,128]{2,1,0:T(8,128)(2,1)} fusion(bf16[128,128,128]{2,1,0:T(8,128)(2,1)} %all-gather.3.cloned.1.call-done, s32[1024]{0:T(1024)S(1)} %pad_clamp_fusion.1), kind=kCustom, calls=%fused_computation | custom fusion | bytes 2097280 | tf_op jit(solution)/shard_map/jit(_take)/gather | solution.py:30
  81.5 113.8 %all-gather.5.cloned.1.call-done = bf16[1536,3072]{1,0:T(8,128)(2,1)} async-done(((bf16[96,3072]{1,0:T(8,128)(2,1)}), bf16[1536,3072]{1,0:T(8,128)(2,1)}) %all-gather.5.cloned.1.call-update) | async-done | bytes 9437200 | tf_op jit(solution)/shard_map/all_gather | solution.py:18
  195.3 9.9 %copy_bitcast_fusion = bf16[1536,24,128]{2,0,1:T(8,128)(2,1)} fusion(bf16[1536,3072]{1,0:T(8,128)(2,1)} %all-gather.5.cloned.1.call-done), kind=kLoop, calls=%fused_computation.3 | loop fusion | bytes 18874368 | tf_op jit(solution)/shard_map/reshape | solution.py:19
  205.2 4.4 %gather_fusion.1 = bf16[2,1536,128]{2,1,0:T(8,128)(2,1)S(1)} fusion(bf16[1536,24,128]{2,0,1:T(8,128)(2,1)} %copy_bitcast_fusion, s32[1024]{0:T(1024)S(1)} %pad_clamp_fusion), kind=kCustom, calls=%fused_computation.1 | custom fusion | bytes 1572872 | tf_op jit(solution)/shard_map/jit(_take)/gather | solution.py:20
  209.6 6.5 %fusion.2 = bf16[2,3072,128]{1,2,0:T(8,128)(2,1)S(1)} fusion(bf16[1536,3072]{1,0:T(8,128)(2,1)} %all-gather.5.cloned.1.call-done, bf16[2,1536,128]{2,1,0:T(8,128)(2,1)S(1)} %gather_fusion.1, pred[2]{0:T(512)(128)(4,1)S(1)} %compare_and_fusion), kind=kOutput, calls=%fused_computation.6 | convolution fusion | flops 2416312320 | bytes 11796482 | tf_op jit(solution)/shard_map/qv,qob->ovb/dot_general | solution.py:21
  216.1 0.9 copy.17
  217.0 0.8 gather_fusion.2
  217.8 2.4 %fusion.5 = bf16[2,128,128]{2,1,0:T(8,128)(2,1)} fusion(bf16[2,16,128,128]{3,2,1,0:T(8,128)(2,1)S(1)} %bitcast.33, bf16[2,16,128,128]{3,2,1,0:T(8,128)(2,1)} %bitcast.32, pred[2,16]{1,0:T(4,128)(4,1)S(1)} %get-tuple-element.5, pred[2,16]{1,0:T(4,128)(4,1)S(1)} %get-tuple-element.6), kind=kOutput, calls=%fused_computation.9 | convolution fusion | flops 135299072 | bytes 2162752 | tf_op jit(solution)/shard_map/okac,okcb->oab/dot_general | solution.py:32
  (4 shorter events, 0.0 us)
Async XLA Ops:
  6.5 71.1 %all-gather.3.cloned.1.call-start = ((), (), s32[]{:S(2)}) async-start(), calls=%async_computation | async-start | bytes 4325376 | tf_op jit(solution)/shard_map/all_gather | solution.py:29
  7.3 188.0 %all-gather.5.cloned.1.call-start = ((), (), s32[]{:S(2)}) async-start(), calls=%async_computation.1 | async-start | bytes 10027008 | tf_op jit(solution)/shard_map/all_gather | solution.py:18
Sparse Core Ops, SparseCore 0:
  10.5 67.0 all-gather.2
  79.7 115.5 all-gather.4
where the time goes:
time: 227 us
  waiting for transfers between devices  181 us (80%)
  local copies, waits for them, and re-layouts  21.2 us (9%)
  between operations  13.5 us (6%)
  matrix products  8.9 us (4%)
  other arithmetic  2.72 us (1%)
    all_gather x1, waiting for transfers between devices, body(): shard_rows = lax.all_gather(df_factors, 'aux', axis=0, tiled=True)  114 us
    all_gather x1, waiting for transfers between devices, body(): all_tiles = lax.all_gather(amplitudes, 'tile', axis=0, tiled=True)  65.5 us
    reshape x1, local copies, waits for them, and re-layouts, body(): columns = shard_rows.reshape(shard_rows.shape[0], ptiles, tile_size)  9.91 us
    dot_general x1, matrix products, body(): jnp.einsum('qv,qob->ovb', shard_rows, right_side, preferred_element_type=...  6.51 us
  transfers between devices with their start and end apart: 2, of which 2 were waited for; matrix products, arithmetic and copies ran while one was open for 3% of the time, Pallas kernels for 0%

commit v1 on v0

--- a/solution.py
+++ b/solution.py
@@ -15,7 +15,9 @@
     pair_width = df_factors.shape[1]
     ptiles = pair_width // tile_size
     per_device = out_count * pair_count
-    shard_rows = lax.all_gather(df_factors, "aux", axis=0, tiled=True)
+    shard_rows = jnp.concatenate(
+        lax.all_to_all(jnp.stack([df_factors] * lax.axis_size("aux")), "aux", 0, 0), axis=0
+    )
     columns = shard_rows.reshape(shard_rows.shape[0], ptiles, tile_size)
     right_side = jnp.take(columns, out_tiles, axis=1)
     assembled = jnp.einsum(

time: 227 us -> 477 us (2.10)
  waiting for transfers between devices: 181 us -> 402 us
  starting transfers between devices: 0.04 us -> 16 us
  local copies, waits for them, and re-layouts: 21.2 us -> 35.7 us
    all_to_all x0 -> x1, waiting for transfers between devices: none -> 335 us  [body(): lax.all_to_all(jnp.stack([df_factors] * lax.axis_size('aux')), 'aux', 0, 0)]
    all_gather x1 -> x0, waiting for transfers between devices: 114 us -> none  [body(): shard_rows = lax.all_gather(df_factors, 'aux', axis=0, tiled=True)]
    all_to_all x0 -> x1, starting transfers between devices: none -> 15.9 us  [body(): lax.all_to_all(jnp.stack([df_factors] * lax.axis_size('aux')), 'aux', 0, 0)]
    another operation x0 -> x2, local copies, waits for them, and re-layouts: none -> 15.4 us  [the longest x1 9.45 us: body(): columns = shard_rows.reshape(shard_rows.shape[0], ptiles, tile_size)]
    reshape x1 -> x0, local copies, waits for them, and re-layouts: 9.91 us -> none  [body(): columns = shard_rows.reshape(shard_rows.shape[0], ptiles, tile_size)]
    unnamed x1 -> x8, local copies, waits for them, and re-layouts: 1.03 us -> 10 us
  transfers between devices with their start and end apart: 2 -> 2, of which waited for: 2 -> 2; matrix products, arithmetic and copies ran while one was open for 3% -> 1% of each run, Pallas kernels for 0% -> 0%
where the time goes in v1:
time: 477 us; the launch traced here: 476 us
  waiting for transfers between devices  402 us (84%)
  local copies, waits for them, and re-layouts  35.7 us (7%)
  starting transfers between devices  16 us (3%)
  between operations  13.5 us (3%)
  matrix products  8.89 us (2%)
    all_to_all x1, waiting for transfers between devices, body(): lax.all_to_all(jnp.stack([df_factors] * lax.axis_size('aux')), 'aux', 0, 0)  335 us
    all_gather x1, waiting for transfers between devices, body(): all_tiles = lax.all_gather(amplitudes, 'tile', axis=0, tiled=True)  65.9 us
    all_to_all x1, starting transfers between devices, body(): lax.all_to_all(jnp.stack([df_factors] * lax.axis_size('aux')), 'aux', 0, 0)  15.9 us
    unnamed x8, local copies, waits for them, and re-layouts  10 us
  transfers between devices with their start and end apart: 2, of which 2 were waited for; matrix products, arithmetic and copies ran while one was open for 1% of the time, Pallas kernels for 0%

profile of v1, /device:TPU:1, one launch (start us, length us, event | category | flops | bytes accessed | tf_op | source)
XLA Modules:
  0.0 476.0 jit_solution(11721659632497930624)
XLA Ops:
  6.5 5.9 %stack.2 = bf16[16,96,3072]{2,1,0:T(8,128)(2,1)} broadcast(bf16[96,3072]{1,0:T(8,128)(2,1)} %param.6), dimensions={1,2} | broadcast | bytes 10027008 | tf_op jit(solution)/shard_map/stack | solution.py:19
  12.4 0.0 copy-start.1
  12.5 0.0 copy-start
  12.5 0.0 copy-start.2
  12.5 15.9 %all-to-all-start = ((bf16[16,96,3072]{2,1,0:T(8,128)(2,1)}), bf16[16,96,3072]{2,1,0:T(8,128)(2,1)}, u32[]{:S(2)}, u32[]{:S(2)}) async-start(bf16[16,96,3072]{2,1,0:T(8,128)(2,1)} %stack.2), calls=%async_computation | async-start | bytes 18874368 | tf_op jit(solution)/shard_map/all_to_all | solution.py:19
  28.4 0.0 all-gather.2.cloned.1.call-start
  28.4 0.7 all-gather.2.cloned.1.call-update
  29.1 0.0 copy-done.1
  29.1 0.1 reshape.96
  29.2 0.0 copy-done
  29.2 0.2 copy.14
  29.4 0.1 reshape.76
  29.6 0.1 squeeze.8
  29.7 0.0 copy-done.2
  29.8 65.9 %all-gather.2.cloned.1.call-done = bf16[128,128,128]{2,1,0:T(8,128)(2,1)} async-done(((bf16[4,128,128]{2,1,0:T(8,128)(2,1)}), bf16[128,128,128]{2,1,0:T(8,128)(2,1)}) %all-gather.2.cloned.1.call-update) | async-done | bytes 4194320 | tf_op jit(solution)/shard_map/all_gather | solution.py:31
  95.7 3.9 gather_fusion
  99.6 335.3 %all-to-all-done = bf16[16,96,3072]{2,1,0:T(8,128)(2,1)} async-done(((bf16[16,96,3072]{2,1,0:T(8,128)(2,1)}), bf16[16,96,3072]{2,1,0:T(8,128)(2,1)}, u32[]{:S(2)}, u32[]{:S(2)}) %all-to-all-start) | async-done | bytes 9437216 | tf_op jit(solution)/shard_map/all_to_all | solution.py:19
  434.9 9.8 %copy.21 = bf16[192,8,24,128]{3,2,1,0:T(8,128)(2,1)} copy(bf16[192,8,24,128]{3,1,2,0:T(8,128)(2,1)} %bitcast.14) | data formatting | bytes 18874368
  444.7 9.4 %copy.15 = bf16[1536,24,128]{2,0,1:T(8,128)(2,1)} copy(bf16[1536,24,128]{2,1,0:T(8,128)(2,1)} %bitcast.28) | data formatting | bytes 18874368 | tf_op jit(solution)/shard_map/reshape;reshape | solution.py:21
  454.1 4.4 gather_fusion.1
  458.6 6.5 %convolution_bitcast_fusion = bf16[2,3072,128]{1,2,0:T(8,128)(2,1)S(1)} fusion(bf16[1536,3072,1]{1,0,2:T(8,128)(2,1)} %bitcast.5, bf16[2,1536,128]{2,1,0:T(8,128)(2,1)S(1)} %gather_fusion.1, pred[2]{0:T(512)(128)(4,1)S(1)} %compare_and_fusion), kind=kOutput, calls=%fused_computation.3 | convolution fusion | flops 2416312320 | bytes 11796482 | tf_op jit(solution)/shard_map/qv,qob->ovb/dot_general | solution.py:23
  465.1 0.9 copy.20
  466.0 0.8 gather_fusion.2
  466.8 2.4 fusion
  (8 shorter events, 0.1 us)
Async XLA Ops:
  12.4 16.7 %copy-start.1 = (s32[2,16]{1,0:T(2,128)S(1)}, s32[2,16]{1,0:T(2,128)}, u32[]{:S(2)}) copy-start(s32[2,16]{1,0:T(2,128)} %param.8) | copy-start | bytes 388
  12.5 16.8 %copy-start = (s32[1024,16]{0,1:T(8,128)S(1)}, s32[1024,16]{0,1:T(8,128)}, u32[]{:S(2)}) copy-start(s32[1024,16]{0,1:T(8,128)} %param.9) | copy-start | bytes 196612
  12.5 17.3 %copy-start.2 = (s32[2]{0:T(128)S(1)}, s32[2]{0:T(128)}, u32[]{:S(2)}) copy-start(s32[2]{0:T(128)} %param.7) | copy-start | bytes 28
  12.5 422.4 %all-to-all-start = ((bf16[16,96,3072]{2,1,0:T(8,128)(2,1)}), bf16[16,96,3072]{2,1,0:T(8,128)(2,1)}, u32[]{:S(2)}, u32[]{:S(2)}) async-start(bf16[16,96,3072]{2,1,0:T(8,128)(2,1)} %stack.2), calls=%async_computation | async-start | bytes 18874368 | tf_op jit(solution)/shard_map/all_to_all | solution.py:19
  28.4 67.3 %all-gather.2.cloned.1.call-start = ((), (), s32[]{:S(2)}) async-start(), calls=%async_computation.1 | async-start | bytes 4325376 | tf_op jit(solution)/shard_map/all_gather | solution.py:31
Sparse Core Ops, SparseCore 0:
  32.4 63.3 all-gather.1
